TPU v7x, 32 devices: a whole 2x2x4 slice. The times are simulated.
32 devices in a mesh: slab: 8 (over z, y), energy: 4 (over x, core).
Axes of the slice: x: 2, y: 2, z: 4, core: 2. Of those that a mesh axis runs over, the one named last changes fastest.
Arguments:
- source: float32 [16, 2, 8, 192, 128], P('slab', None, 'energy'), may hold values from -1.2 to 1.2
- onsite_block: float32 [192, 192], replicated, may hold values from -1.3 to 1.3, as said below
- hopping_block: float32 [192, 192], replicated, may hold values from -0.5 to 1.5
- potential_table: float32 [16, 192], replicated, may hold values from -0.5 to 0.5
- slab_profile: int32 [16], P('slab'), may hold values from 0 to 15
- occupation: float32 [16, 8, 192], P('slab', 'energy'), may hold values from 0.1 to 1
- coupling: float32 [4], replicated, may hold values from 0.02 to 0.08
- phonon_shift: int32 [4], replicated, may hold values from 1 to 2, as said below
Outputs:
- amplitude: float32 [16, 2, 8, 192, 128], P('slab', None, 'energy')
- density: float32 [16, 8, 192], P('slab', 'energy')
Inputs may be any that keep to these rules, and one draw needn't show every extreme that they name: `phonon_shift`: some mode shifts by exactly 2 points and some by exactly 1. `onsite_block`: symmetric.
All inputs are finite; a program needn't handle non-finite values.
Results may differ from a plain program's by a relative error of at most 0.0003.
Values sent between devices are 32-bit elements; how exact they have to be, the bound alone decides.
A program may use at most 128 MiB of HBM per device.

v0:
```python
import functools

import jax
import jax.numpy as jnp
from jax import lax
from jax.experimental import pallas as pl
from jax.experimental.pallas import tpu as pltpu
from jax.sharding import PartitionSpec as P

broadening = 0.05
energy_low = -1.2
energy_step = 0.15


def padded(block, sides, width):
    for axis, dim in sides:
        count = lax.axis_size(axis)
        forward = [(i, i + 1) for i in range(count - 1)]
        backward = [(target, source) for source, target in forward]
        low = lax.ppermute(
            lax.slice_in_dim(block, block.shape[dim] - width, None, axis=dim), axis, forward
        )
        high = lax.ppermute(lax.slice_in_dim(block, 0, width, axis=dim), axis, backward)
        block = jnp.concatenate([low, block, high], axis=dim)
    return block


def shifted(array, axis, by):
    count = lax.axis_size(axis)
    pairs = [(i, i + by) for i in range(count) if 0 <= i + by < count]
    return lax.ppermute(array, axis, pairs)


def swapped(array, axis):
    count = lax.axis_size(axis)
    return lax.ppermute(array, axis, [(i, i ^ 1) for i in range(count)])


def matmul_exact(left, right):
    return jnp.matmul(left, right, precision=lax.Precision.HIGHEST)


def halves(value):
    high = value.astype(jnp.bfloat16)
    return high, (value - high.astype(jnp.float32)).astype(jnp.bfloat16)


def dot_rows(left, right):
    return lax.dot_general(
        left, right, (((0,), (0,)), ((), ())), preferred_element_type=jnp.float32
    )


def complex_dot_rows(left_real, left_imag, right_real, right_imag):
    lrh, lrl = halves(left_real)
    lih, lil = halves(left_imag)
    rrh, rrl = halves(right_real)
    rih, ril = halves(right_imag)
    right = jnp.concatenate([rrh, rrl, rrh, rih, ril, rih], axis=0)
    for_real = jnp.concatenate([lrh, lrh, lrl, -lih, -lih, -lil], axis=0)
    for_imag = jnp.concatenate([lih, lih, lil, lrh, lrh, lrl], axis=0)
    return dot_rows(for_real, right), dot_rows(for_imag, right)


def dot_split(left, right):
    lh, ll = left
    rh, rl = right
    dot = functools.partial(jnp.dot, preferred_element_type=jnp.float32)
    return dot(lh, rh) + (dot(lh, rl) + dot(ll, rh))


def real_dot(left, right):
    split = halves(left)
    return tuple(dot_split(split, halves(part)) for part in right)


def dot_real(left, right):
    split = halves(right)
    return tuple(dot_split(halves(part), split) for part in left)


def complex_dot(left, right):
    lr, li = halves(left[0]), halves(left[1])
    rr, ri = halves(right[0]), halves(right[1])
    return (
        dot_split(lr, rr) - dot_split(li, ri),
        dot_split(lr, ri) + dot_split(li, rr),
    )


def plus(left, right):
    return left[0] + right[0], left[1] + right[1]


def minus(left, right):
    return left[0] - right[0], left[1] - right[1]


def negative(value):
    return -value[0], -value[1]


def turned(value):
    return value[0].T, value[1].T


def take(ref, *index):
    return ref[(0,) + index], ref[(1,) + index]


def put(ref, value, *index):
    ref[(0,) + index] = value[0]
    ref[(1,) + index] = value[1]


def invert_small(blocks):
    size = blocks[0][0].shape[0]
    panel = 4 if size % 4 == 0 else 1
    lane = lax.broadcasted_iota(jnp.int32, (1, size), 1)
    row = lax.broadcasted_iota(jnp.int32, (size, 1), 0)
    for start in range(0, size, panel):
        spread = [
            [
                tuple(
                    jnp.broadcast_to(part[:, k : k + 1], (size, size)) for part in parts
                )
                for k in range(start, start + panel)
            ]
            for parts in blocks
        ]
        for at in range(panel):
            k = start + at
            at_lane = lane == k
            at_row = row == k
            after = []
            for (real, imag), columns in zip(blocks, spread):
                col_real, col_imag = columns[at]
                pivot_real = col_real[k : k + 1]
                pivot_imag = col_imag[k : k + 1]
                scale = 1.0 / (pivot_real * pivot_real + pivot_imag * pivot_imag)
                inv_real = pivot_real * scale
                inv_imag = -pivot_imag * scale
                for later in range(at + 1, panel):
                    j = start + later
                    entry_real = col_real[j : j + 1]
                    entry_imag = col_imag[j : j + 1]
                    new_real = inv_real * entry_real - inv_imag * entry_imag
                    new_imag = inv_real * entry_imag + inv_imag * entry_real
                    old_real, old_imag = columns[later]
                    columns[later] = (
                        jnp.where(
                            at_row,
                            new_real,
                            old_real - (col_real * new_real - col_imag * new_imag),
                        ),
                        jnp.where(
                            at_row,
                            new_imag,
                            old_imag - (col_real * new_imag + col_imag * new_real),
                        ),
                    )
                row_real = jnp.where(at_lane, 1.0, real[k : k + 1])
                row_imag = jnp.where(at_lane, 0.0, imag[k : k + 1])
                new_real = inv_real * row_real - inv_imag * row_imag
                new_imag = inv_real * row_imag + inv_imag * row_real
                real = jnp.where(at_lane, 0.0, real) - (col_real * new_real - col_imag * new_imag)
                imag = jnp.where(at_lane, 0.0, imag) - (col_real * new_imag + col_imag * new_real)
                real = jnp.where(at_row, new_real, real)
                imag = jnp.where(at_row, new_imag, imag)
                after.append((real, imag))
            blocks = after
    return blocks


def invert_steps(state, batch, size):
    width = state.shape[-1]
    block = next(s for s in (32, 16, 8, 1) if size % s == 0)

    def step(index, carry):
        low = pl.multiple_of(index * block, block)
        lane = lax.broadcasted_iota(jnp.int32, (block, width), 1)
        row = lax.broadcasted_iota(jnp.int32, (block, width), 0)
        inside = (lane >= low) & (lane < low + block)
        unit = jnp.where(lane == row + low, 1.0, 0.0)
        sign = jnp.where(lane < low, -1.0, 1.0)
        back = lax.rem(width - low, width)
        rows = []
        small = []
        for b in range(batch):
            real = state[b, 0, pl.ds(low, block), :]
            imag = state[b, 1, pl.ds(low, block), :]
            rows.append((real, imag))
            small.append(
                (
                    pltpu.roll(real, back, 1)[:, :block],
                    pltpu.roll(imag, back, 1)[:, :block],
                )
            )
        small = invert_small(small)
        all_lane = lax.broadcasted_iota(jnp.int32, (size, width), 1)
        all_inside = (all_lane >= low) & (all_lane < low + block)
        for b in range(batch):
            real, imag = rows[b]
            new_real, new_imag = complex_dot_rows(
                *small[b], jnp.where(inside, unit, real), jnp.where(inside, 0.0, imag)
            )
            change_real, change_imag = complex_dot_rows(
                (sign * real)[:, :size], (sign * imag)[:, :size], new_real, new_imag
            )
            state[b, 0] = jnp.where(all_inside, 0.0, state[b, 0]) - change_real
            state[b, 1] = jnp.where(all_inside, 0.0, state[b, 1]) - change_imag
            state[b, 0, pl.ds(low, block), :] = new_real
            state[b, 1, pl.ds(low, block), :] = new_imag
        return carry

    lax.fori_loop(0, size // block, step, 0)


def invert_all(state, blocks):
    size = blocks[0][0].shape[0]
    for b, parts in enumerate(blocks):
        for part in range(2):
            state[b, part, :, :size] = 0.5 * (parts[part] + parts[part].T)
            if state.shape[-1] > size:
                state[b, part, :, size:] = jnp.zeros(
                    (size, state.shape[-1] - size), jnp.float32
                )
    invert_steps(state, len(blocks), size)
    return [(state[b, 0, :, :size], state[b, 1, :, :size]) for b in range(len(blocks))]


def run(kernel, out_shapes, inputs, size=0, batch=0, micros=2):
    scratch = []
    if batch:
        scratch = [pltpu.VMEM((batch, 2, size, -(-size // 128) * 128), jnp.float32)]
    return pl.pallas_call(
        kernel,
        out_shape=[jax.ShapeDtypeStruct(shape, jnp.float32) for shape in out_shapes],
        in_specs=[pl.BlockSpec(memory_space=pltpu.VMEM)] * len(inputs),
        out_specs=[pl.BlockSpec(memory_space=pltpu.VMEM)] * len(out_shapes),
        scratch_shapes=scratch,
        compiler_params=pltpu.CompilerParams(vmem_limit_bytes=48 * 1024 * 1024),
        cost_estimate=pl.CostEstimate(
            flops=micros * 1000000000, bytes_accessed=1000000, transcendentals=0
        ),
    )(*inputs)


def local_kernel(
    onsite_ref, hop_ref, real_ref, imag_ref,
    g0_ref, g1_ref, g2_ref, below_ref, above_ref, sb_ref, sa_ref,
    out_pivot_ref, out_upper_ref, pivot_ref, lower_ref, state,
):
    count = real_ref.shape[1]
    size = onsite_ref.shape[0]
    eye = lax.broadcasted_iota(jnp.int32, (size, size), 0) == lax.broadcasted_iota(
        jnp.int32, (size, size), 1
    )
    hop = hop_ref[...]
    hop_t = hop.T

    def block(slab, e):
        return (
            jnp.where(eye, real_ref[slab, e : e + 1, :], 0.0) - onsite_ref[...],
            jnp.where(eye, imag_ref[slab, e : e + 1, :], 0.0),
        )

    pairs = invert_all(
        state, [block(0, e) for e in range(count)] + [block(2, e) for e in range(count)]
    )
    middle = []
    for e in range(count):
        g0, g2 = pairs[e], pairs[count + e]
        put(g0_ref, g0, e)
        put(g2_ref, g2, e)
        g0h, g0t = dot_real(g0, hop), dot_real(g0, hop_t)
        g2h, g2t = dot_real(g2, hop), dot_real(g2, hop_t)
        put(below_ref, negative(real_dot(hop_t, g0t)), e)
        put(above_ref, negative(real_dot(hop, g2h)), e)
        put(out_pivot_ref, negative(real_dot(hop, g0t)), e)
        put(pivot_ref, minus(block(3, e), real_dot(hop_t, g2h)), e)
        middle.append(minus(block(1, e), plus(real_dot(hop_t, g0h), real_dot(hop, g2t))))
    for e, g1 in enumerate(invert_all(state, middle)):
        put(g1_ref, g1, e)
        below, above = take(below_ref, e), take(above_ref, e)
        below_t, above_t = turned(below), turned(above)
        sb = complex_dot(g1, below)
        sa = complex_dot(g1, above)
        put(sb_ref, sb, e)
        put(sa_ref, sa, e)
        put(out_pivot_ref, minus(take(out_pivot_ref, e), complex_dot(below_t, sb)), e)
        put(pivot_ref, minus(take(pivot_ref, e), complex_dot(above_t, sa)), e)
        lower = negative(complex_dot(above_t, sb))
        put(lower_ref, lower, e)
        put(out_upper_ref, turned(lower), e)


def local_right_kernel(
    hop_ref, g0_ref, g1_ref, g2_ref, below_ref, above_ref, right_ref,
    z0_ref, z1_ref, z2_ref, out_ref, own_ref,
):
    hop = hop_ref[...]
    hop_t = hop.T
    for e in range(g0_ref.shape[1]):
        b0, b1, b2, b3 = (
            (right_ref[slab, 0, e], right_ref[slab, 1, e]) for slab in range(4)
        )
        z0 = complex_dot(take(g0_ref, e), b0)
        z2 = complex_dot(take(g2_ref, e), b2)
        b1 = plus(b1, plus(real_dot(hop_t, z0), real_dot(hop, z2)))
        z1 = complex_dot(take(g1_ref, e), b1)
        put(z0_ref, z0, e)
        put(z1_ref, z1, e)
        put(z2_ref, z2, e)
        put(
            out_ref,
            minus(real_dot(hop, z0), complex_dot(turned(take(below_ref, e)), z1)),
            e,
        )
        put(
            own_ref,
            minus(
                plus(b3, real_dot(hop_t, z2)), complex_dot(turned(take(above_ref, e)), z1)
            ),
            e,
        )


def first_kernel(own_ref, more_ref, pivot_ref, g_ref, state):
    count = own_ref.shape[1]
    for e in range(count):
        put(pivot_ref, plus(take(own_ref, e), take(more_ref, e)), e)
    inverse = invert_all(state, [take(pivot_ref, e) for e in range(count)])
    for e in range(count):
        put(g_ref, inverse[e], e)


def level_kernel(old_ref, lower_ref, upper_ref, below_ref, above_ref, pivot_ref, g_ref, state):
    count = old_ref.shape[1]
    for e in range(count):
        change = plus(
            complex_dot(take(lower_ref, e), take(below_ref, e)),
            complex_dot(take(upper_ref, e), take(above_ref, e)),
        )
        put(pivot_ref, minus(take(old_ref, e), change), e)
    inverse = invert_all(state, [take(pivot_ref, e) for e in range(count)])
    for e in range(count):
        put(g_ref, inverse[e], e)


def scale_kernel(g_ref, lower_ref, upper_ref, xl_ref, xu_ref):
    for e in range(g_ref.shape[1]):
        g = take(g_ref, e)
        put(xl_ref, complex_dot(g, take(lower_ref, e)), e)
        put(xu_ref, complex_dot(g, take(upper_ref, e)), e)


def product_kernel(left_ref, right_ref, out_ref):
    for e in range(left_ref.shape[1]):
        put(out_ref, complex_dot(take(left_ref, e), take(right_ref, e)), e)


def coupling_kernel(lower_ref, upper_ref, below_ref, above_ref, new_lower_ref, new_upper_ref):
    for e in range(lower_ref.shape[1]):
        put(new_lower_ref, negative(complex_dot(take(lower_ref, e), take(below_ref, e))), e)
        put(new_upper_ref, negative(complex_dot(take(upper_ref, e), take(above_ref, e))), e)


def right_kernel(
    g_ref, lower_ref, upper_ref, below_ref, above_ref, right_ref, new_ref, x_ref
):
    for e in range(lower_ref.shape[1]):
        change = plus(
            complex_dot(take(lower_ref, e), take(below_ref, e)),
            complex_dot(take(upper_ref, e), take(above_ref, e)),
        )
        new = minus(take(right_ref, e), change)
        put(new_ref, new, e)
        put(x_ref, complex_dot(take(g_ref, e), new), e)


def middle_kernel(z1_ref, sb_ref, sa_ref, previous_ref, x3_ref, x1_ref):
    for e in range(z1_ref.shape[1]):
        change = plus(
            complex_dot(take(sb_ref, e), take(previous_ref, e)),
            complex_dot(take(sa_ref, e), take(x3_ref, e)),
        )
        put(x1_ref, minus(take(z1_ref, e), change), e)


def outer_kernel(
    hop_ref, g0_ref, g2_ref, z0_ref, z2_ref, previous_ref, x1_ref, x3_ref, x0_ref, x2_ref
):
    hop = hop_ref[...]
    hop_t = hop.T
    for e in range(z0_ref.shape[1]):
        x1 = take(x1_ref, e)
        for_0 = plus(real_dot(hop_t, take(previous_ref, e)), real_dot(hop, x1))
        for_2 = plus(real_dot(hop_t, x1), real_dot(hop, take(x3_ref, e)))
        put(x0_ref, plus(take(z0_ref, e), complex_dot(take(g0_ref, e), for_0)), e)
        put(x2_ref, plus(take(z2_ref, e), complex_dot(take(g2_ref, e), for_2)), e)


def per_device(
    source,
    onsite_block,
    hopping_block,
    potential_table,
    slab_profile,
    occupation,
    coupling,
    phonon_shift,
):
    slab_count = occupation.shape[0]
    energy_count = occupation.shape[1]
    orbitals = onsite_block.shape[0]
    half = energy_count // 2
    if slab_count != 2 or energy_count % 2 or lax.axis_size("slab") % 2:
        raise ValueError("unsupported shape")
    hop = hopping_block
    place = lax.axis_index("slab")
    upper_half = (place % 2) == 1
    widened = padded(occupation, (("energy", 1),), energy_count)
    own_points = jnp.arange(energy_count, dtype=jnp.int32)[:, None]
    all_points = jnp.arange(3 * energy_count, dtype=jnp.int32)[None, :]
    weights = jnp.zeros((energy_count, 3 * energy_count), jnp.float32)
    for mode in range(phonon_shift.shape[0]):
        above = (all_points == own_points + energy_count + phonon_shift[mode]).astype(jnp.float32)
        below = (all_points == own_points + energy_count - phonon_shift[mode]).astype(jnp.float32)
        weights = weights + coupling[mode] * (above + below)
    damping = jnp.einsum("ek,skb->seb", weights, widened, precision=lax.Precision.HIGHEST)
    chosen = (
        slab_profile[:, None] == jnp.arange(potential_table.shape[0], dtype=jnp.int32)[None, :]
    ).astype(jnp.float32)
    potential = matmul_exact(chosen, potential_table)

    def exchanged(array, axis):
        low = lax.slice_in_dim(array, 0, half, axis=axis)
        high = lax.slice_in_dim(array, half, energy_count, axis=axis)
        kept = jnp.where(upper_half, high, low)
        other = swapped(jnp.where(upper_half, low, high), "slab")
        return kept, other

    def ordered(kept, other):
        return jnp.where(
            upper_half,
            jnp.concatenate([other, kept], axis=0),
            jnp.concatenate([kept, other], axis=0),
        )

    shared = jnp.concatenate(
        [damping, jnp.broadcast_to(potential[:, None], damping.shape)], axis=-1
    )
    shared = ordered(*exchanged(shared, 1))
    damping = shared[..., :orbitals]
    potential = shared[..., orbitals:]
    right = ordered(*exchanged(source, 2))

    first_point = lax.axis_index("energy") * energy_count + jnp.where(upper_half, half, 0)
    energies = energy_low + energy_step * (
        first_point + jnp.arange(half, dtype=jnp.int32)
    ).astype(jnp.float32)
    real_diag = energies[None, :, None] - potential
    imag_diag = broadening + damping
    square = (2, half, orbitals, orbitals)
    tall = (2, half, orbitals, source.shape[-1])
    g0, g1, g2, below, above, sb, sa, out_pivot, out_upper, pivot, lower = run(
        local_kernel,
        [square] * 11,
        [onsite_block, hop, real_diag, imag_diag],
        orbitals,
        2 * half,
        30,
    )
    more = shifted(out_pivot, "slab", -2)
    z0, z1, z2, out_right, right_now = run(
        local_right_kernel, [tall] * 5, [hop, g0, g1, g2, below, above, right]
    )
    upper = shifted(out_upper, "slab", -2)
    right_now = (right_now, shifted(out_right, "slab", -2))
    count = lax.axis_size("slab") // 2
    pivot, inverse = run(first_kernel, [square] * 2, [pivot, more], orbitals, half, 14)
    right_now = right_now[0] + right_now[1]
    scaled_right = None
    for level in range((count - 1).bit_length()):
        distance = 2 << level
        last = distance >= count
        x_lower, x_upper = run(scale_kernel, [square] * 2, [inverse, lower, upper])
        below_upper = shifted(x_upper, "slab", distance)
        above_lower = shifted(x_lower, "slab", -distance)
        if scaled_right is None:
            (scaled_right,) = run(product_kernel, [tall], [inverse, right_now])
        if not last:
            below_lower = shifted(x_lower, "slab", distance)
            above_upper = shifted(x_upper, "slab", -distance)
        below_right = shifted(scaled_right, "slab", distance)
        above_right = shifted(scaled_right, "slab", -distance)
        pivot, inverse = run(
            level_kernel,
            [square] * 2,
            [pivot, lower, upper, below_upper, above_lower],
            orbitals,
            half,
            14,
        )
        right_now, scaled_right = run(
            right_kernel,
            [tall] * 2,
            [inverse, lower, upper, below_right, above_right, right_now],
        )
        if not last:
            lower, upper = run(
                coupling_kernel, [square] * 2, [lower, upper, below_lower, above_upper]
            )
    if scaled_right is None:
        (scaled_right,) = run(product_kernel, [tall], [inverse, right_now])
    x3 = scaled_right
    previous = shifted(x3, "slab", 2)
    (x1,) = run(middle_kernel, [tall], [z1, sb, sa, previous, x3])
    first = swapped(jnp.where(upper_half, x1, x3), "slab")
    x0, x2 = run(outer_kernel, [tall] * 2, [hop, g0, g2, z0, z2, previous, x1, x3])
    second = swapped(jnp.where(upper_half, x0, x2), "slab")
    kept = jnp.where(upper_half, jnp.stack([x2, x3]), jnp.stack([x0, x1]))
    other = jnp.stack([second, first])
    amplitude = jnp.where(
        upper_half,
        jnp.concatenate([other, kept], axis=2),
        jnp.concatenate([kept, other], axis=2),
    )
    density = jnp.sum(amplitude[:, 0] ** 2 + amplitude[:, 1] ** 2, axis=-1)
    return (amplitude, density)


def solution(mesh):
    placed = (
        P("slab", None, "energy", None, None),
        P(),
        P(),
        P(),
        P("slab"),
        P("slab", "energy", None),
        P(),
        P(),
    )
    return jax.shard_map(
        per_device,
        mesh=mesh,
        in_specs=placed,
        out_specs=(P("slab", None, "energy", None, None), P("slab", "energy", None)),
        check_vma=False,
    )
```

profile of v0, /device:TPU:0, one launch (start us, length us, event | category | flops | bytes accessed | tf_op | source)
XLA Modules:
  0.0 177.7 jit_solution(10597744634387250666)
XLA Ops:
  0.6 2.4 %collective-permute-start = (f32[2,2,192]{2,1,0:T(2,128)}, f32[2,2,192]{2,1,0:T(2,128)S(1)}, u32[]{:S(2)}, u32[]{:S(2)}) collective-permute-start(f32[2,2,192]{2,1,0:T(2,128)} %param.13), channel_id=1, source_target_pairs={{0,1},{1,2},{2,3},{4,5},{5,6},{6,7},{8,9},{9,10},{10,11},{12,13},{... | collective-permute-start | bytes 9224 | tf_op jit(solution)/shard_map/ppermute | solution.py:20
  3.0 1.3 collective-permute-start.1
  4.3 1.5 fusion.54
  5.8 0.6 fusion.55
  6.4 0.6 fusion.50
  7.0 0.7 fusion.48
  8.5 0.6 fusion.46
  9.2 0.7 copy-done.5
  9.9 2.7 %convolution_bitcast_fusion = f32[2,2,192]{2,1,0:T(2,128)S(1)} fusion(f32[2,2,192]{2,1,0:T(2,128)S(1)} %collective-permute-done.1, f32[2,2,192]{2,1,0:T(2,128)S(1)} %copy-done.5, f32[2,2,192]{2,1,0:T(2,128)S(1)} %collective-permute-done, s32[2]{0:T(128)S(1)} %get-tuple-element.82, s32[2]{0:T(128)S(1)} %get-tuple-element.83, f32[]{:T(128)} %bitcast.6, ...), kind=kOutput, calls=%fused_computation | convolution fusion | flops 60228 | bytes 12368 | tf_op jit(solution)/shard_map/ek,skb->seb/dot_general | solution.py:431
  12.7 2.4 %collective-permute-start.2 = (f32[2,1,384]{2,1,0:T(1,128)S(1)}, f32[2,1,384]{2,1,0:T(1,128)S(1)}, u32[]{:S(2)}, u32[]{:S(2)}) collective-permute-start(f32[2,1,384]{2,1,0:T(1,128)S(1)} %get-tuple-element.70), channel_id=1, source_target_pairs={{0,4},{4,0},{8,12},{12,8},{16,20},{20,16},{24,28},{28,24},{1,5},{5... | collective-permute-start | bytes 9224 | tf_op jit(solution)/shard_map/ppermute | solution.py:36
  15.1 1.6 collective-permute-done.2
  16.8 30.7 %shard_map.95 = (f32[2,1,192,192]{3,2,1,0:T(8,128)S(1)}, f32[2,1,192,192]{3,2,1,0:T(8,128)S(1)}, f32[2,1,192,192]{3,2,1,0:T(8,128)S(1)}, f32[2,1,192,192]{3,2,1,...) custom-call(f32[192,192]{1,0:T(8,128)S(1)} %copy-done.1, ...), custom_call_target="tpu_custom_call" | custom-call | flops 30000001024 | bytes 1000000 | tf_op jit(solution)/shard_map/pallas_call | solution.py:236
  47.5 1.3 collective-permute-start.4
  48.9 2.1 %collective-permute-start.3 = (f32[2,2,1,192,128]{4,3,1,2,0:T(8,128)S(1)}, f32[2,2,1,192,128]{4,3,1,2,0:T(8,128)S(1)}, u32[]{:S(2)}, u32[]{:S(2)}) collective-permute-start(f32[2,2,1,192,128]{4,3,1,2,0:T(8,128)S(1)} %get-tuple-element.68), channel_id=1, source_target_pairs={{0,4},{4,0},{8,12},{12,8},{16,20},{20,16},{24,28},{28,24},{1,5},{5... | collective-permute-start | bytes 1179656 | tf_op jit(solution)/shard_map/ppermute | solution.py:36
  51.0 1.3 collective-permute-start.5
  52.3 8.5 %collective-permute-done.4.more_ref = f32[2,1,192,192]{3,2,1,0:T(8,128)S(1)} collective-permute-done((f32[2,1,192,192]{3,2,1,0:T(8,128)S(1)}, f32[2,1,192,192]{3,2,1,0:T(8,128)S(1)}, u32[]{:S(2)}, u32[]{:S(2)}) %collective-permute-start.4) | collective-permute-done | bytes 294944 | tf_op jit(solution)/shard_map/ppermute | solution.py:31
  60.8 11.7 %shard_map.97 = (f32[2,1,192,192]{3,2,1,0:T(8,128)S(1)}, f32[2,1,192,192]{3,2,1,0:T(8,128)S(1)}) custom-call(f32[2,1,192,192]{3,2,1,0:T(8,128)S(1)} %get-tuple-element.41.own_ref, f32[2,1,192,192]{3,2,1,0:T(8,128)S(1)} %collective-permute-done.4.more_ref), custom_call_target="tpu_custom_call" | custom-call | flops 14000000000 | bytes 1000000 | tf_op jit(solution)/shard_map/pallas_call | solution.py:236
  72.6 2.6 %shard_map.96 = (f32[2,1,192,128]{3,2,1,0:T(8,128)S(1)}, f32[2,1,192,128]{3,2,1,0:T(8,128)S(1)}, f32[2,1,192,128]{3,2,1,0:T(8,128)S(1)}, f32[2,1,192,128]{3,2,1,0:T(8,128)S(1)}, f32[2,1,192,128]{3,2,1,0:T(8,128)S(1)}) custom-call(f32[192,192]{1,0:T(8,128)S(1)} %copy-done.2, f32[2,1,192,192]{3,2,1,0:T(8,128)S(1)} %get-tuple-element.34.g0_ref, ...), custom_call_target="tpu_custom_call" | custom-call | flops 2000000000 | bytes 1000000 | tf_op jit(solution)/shard_map/pallas_call | solution.py:236
  75.2 1.3 collective-permute-start.12
  76.5 0.8 shard_map.98
  77.3 1.3 collective-permute-start.9
  78.6 5.6 %collective-permute-start.8 = (f32[2,1,192,192]{3,2,1,0:T(8,128)S(1)}, f32[2,1,192,192]{3,2,1,0:T(8,128)S(1)}, u32[]{:S(2)}, u32[]{:S(2)}) collective-permute-start(f32[2,1,192,192]{3,2,1,0:T(8,128)S(1)} %get-tuple-element.48), channel_id=1, source_target_pairs={{0,8},{4,12},{8,16},{12,20},{16,24},{20,28},{1,9},{5,13},{9,17},{1... | collective-permute-start | bytes 884744 | tf_op jit(solution)/shard_map/ppermute | solution.py:31
  84.2 3.9 %collective-permute-start.6 = (f32[2,1,192,192]{3,2,1,0:T(8,128)S(1)}, f32[2,1,192,192]{3,2,1,0:T(8,128)S(1)}, u32[]{:S(2)}, u32[]{:S(2)}) collective-permute-start(f32[2,1,192,192]{3,2,1,0:T(8,128)S(1)} %get-tuple-element.47), channel_id=1, source_target_pairs={{0,8},{4,12},{8,16},{12,20},{16,24},{20,28},{1,9},{5,13},{9,17},{1... | collective-permute-start | bytes 884744 | tf_op jit(solution)/shard_map/ppermute | solution.py:31
  88.1 1.5 collective-permute-start.7
  90.1 1.3 collective-permute-start.14
  91.4 2.1 %collective-permute-done.9.above_ref = f32[2,1,192,192]{3,2,1,0:T(8,128)S(1)} collective-permute-done((f32[2,1,192,192]{3,2,1,0:T(8,128)S(1)}, f32[2,1,192,192]{3,2,1,0:T(8,128)S(1)}, u32[]{:S(2)}, u32[]{:S(2)}) %collective-permute-start.9) | collective-permute-done | bytes 294944 | tf_op jit(solution)/shard_map/ppermute | solution.py:31
  93.6 4.0 %collective-permute-start.13 = (f32[2,1,192,128]{3,2,1,0:T(8,128)S(1)}, f32[2,1,192,128]{3,2,1,0:T(8,128)S(1)}, u32[]{:S(2)}, u32[]{:S(2)}) collective-permute-start(f32[2,1,192,128]{3,2,1,0:T(8,128)S(1)} %shard_map.103), channel_id=1, source_target_pairs={{0,8},{4,12},{8,16},{12,20},{16,24},{20,28},{1,9},{5,13},{9,17},{1... | collective-permute-start | bytes 589832 | tf_op jit(solution)/shard_map/ppermute | solution.py:31
  97.6 0.8 shard_map.100
  98.4 3.7 %collective-permute-done.6.below_ref = f32[2,1,192,192]{3,2,1,0:T(8,128)S(1)} collective-permute-done((f32[2,1,192,192]{3,2,1,0:T(8,128)S(1)}, f32[2,1,192,192]{3,2,1,0:T(8,128)S(1)}, u32[]{:S(2)}, u32[]{:S(2)}) %collective-permute-start.6) | collective-permute-done | bytes 294944 | tf_op jit(solution)/shard_map/ppermute | solution.py:31
  102.3 12.5 %shard_map.99 = (f32[2,1,192,192]{3,2,1,0:T(8,128)S(1)}, f32[2,1,192,192]{3,2,1,0:T(8,128)S(1)}) custom-call(f32[2,1,192,192]{3,2,1,0:T(8,128)S(1)} %get-tuple-element.43.old_ref, f32[2,1,192,192]{3,2,1,0:T(8,128)S(1)} %get-tuple-element.44.lower_ref, f32[2,1,192,192]{3,2,1,0:T(8,128)S(1)} %collective-permute-done.5.upper_ref, ...), custom_call_target="tpu_custom_call" | custom-call | flops 14000000000 | bytes 1000000 | tf_op jit(solution)/shard_map/pallas_call | solution.py:236
  114.7 0.8 shard_map.101
  115.5 5.6 %collective-permute-start.10 = (f32[2,1,192,192]{3,2,1,0:T(8,128)S(1)}, f32[2,1,192,192]{3,2,1,0:T(8,128)S(1)}, u32[]{:S(2)}, u32[]{:S(2)}) collective-permute-start(f32[2,1,192,192]{3,2,1,0:T(8,128)S(1)} %get-tuple-element.53), channel_id=1, source_target_pairs={{0,16},{4,20},{8,24},{12,28},{1,17},{5,21},{9,25},{13,29},{2,18},{... | collective-permute-start | bytes 884744 | tf_op jit(solution)/shard_map/ppermute | solution.py:31
  121.1 1.3 collective-permute-start.11
  122.5 1.2 shard_map.104
  123.7 1.3 collective-permute-start.16
  125.0 5.5 %collective-permute-start.15 = (f32[2,1,192,128]{3,2,1,0:T(8,128)S(1)}, f32[2,1,192,128]{3,2,1,0:T(8,128)S(1)}, u32[]{:S(2)}, u32[]{:S(2)}) collective-permute-start(f32[2,1,192,128]{3,2,1,0:T(8,128)S(1)} %get-tuple-element.58), channel_id=1, source_target_pairs={{0,16},{4,20},{8,24},{12,28},{1,17},{5,21},{9,25},{13,29},{2,18},{... | collective-permute-start | bytes 589832 | tf_op jit(solution)/shard_map/ppermute | solution.py:31
  130.5 17.0 %collective-permute-done.11.above_ref = f32[2,1,192,192]{3,2,1,0:T(8,128)S(1)} collective-permute-done((f32[2,1,192,192]{3,2,1,0:T(8,128)S(1)}, f32[2,1,192,192]{3,2,1,0:T(8,128)S(1)}, u32[]{:S(2)}, u32[]{:S(2)}) %collective-permute-start.11) | collective-permute-done | bytes 294944 | tf_op jit(solution)/shard_map/ppermute | solution.py:31
  147.5 12.5 %shard_map.102 = (f32[2,1,192,192]{3,2,1,0:T(8,128)}, f32[2,1,192,192]{3,2,1,0:T(8,128)S(1)}) custom-call(f32[2,1,192,192]{3,2,1,0:T(8,128)S(1)} %get-tuple-element.49.old_ref, f32[2,1,192,192]{3,2,1,0:T(8,128)S(1)} %get-tuple-element.50.lower_ref, f32[2,1,192,192]{3,2,1,0:T(8,128)S(1)} %get-tuple-element.51.upper_ref, ...), custom_call_target="tpu_custom_call" | custom-call | flops 14000000000 | bytes 1000000 | tf_op jit(solution)/shard_map/pallas_call | solution.py:236
  160.0 1.7 shard_map.105
  161.7 1.3 collective-permute-start.17
  163.0 3.2 %collective-permute-done.17.previous_ref = f32[2,1,192,128]{3,2,1,0:T(8,128)S(1)} collective-permute-done((f32[2,1,192,128]{3,2,1,0:T(8,128)S(1)}, f32[2,1,192,128]{3,2,1,0:T(8,128)S(1)}, u32[]{:S(2)}, u32[]{:S(2)}) %collective-permute-start.17) | collective-permute-done | bytes 196640 | tf_op jit(solution)/shard_map/ppermute | solution.py:31
  166.1 0.8 shard_map.106.x1_ref
  167.0 1.6 collective-permute-start.19
  168.5 1.4 shard_map.107
  170.6 3.2 %collective-permute-done.19 = f32[2,1,192,128]{3,2,0,1:T(8,128)S(1)} collective-permute-done((f32[2,1,192,128]{3,2,0,1:T(8,128)S(1)}, f32[2,1,192,128]{3,2,0,1:T(8,128)S(1)}, u32[]{:S(2)}, u32[]{:S(2)}) %collective-permute-start.19) | collective-permute-done | bytes 196640 | tf_op jit(solution)/shard_map/ppermute | solution.py:36
  173.8 2.1 %collective-permute-done.18 = f32[2,1,192,128]{3,2,0,1:T(8,128)S(1)} collective-permute-done((f32[2,1,192,128]{3,2,0,1:T(8,128)S(1)}, f32[2,1,192,128]{3,2,0,1:T(8,128)S(1)}, u32[]{:S(2)}, u32[]{:S(2)}) %collective-permute-start.18) | collective-permute-done | bytes 196640 | tf_op jit(solution)/shard_map/ppermute | solution.py:36
  176.0 0.8 fusion.2
  176.8 0.9 copy.17
  (40 shorter events, 2.5 us)
Async XLA Ops:
  0.6 7.7 %copy-start = (f32[16,192]{1,0:T(8,128)S(1)}, f32[16,192]{1,0:T(8,128)}, u32[]{:S(2)}) copy-start(f32[16,192]{1,0:T(8,128)} %param.11) | copy-start | bytes 36868
  0.6 8.6 %collective-permute-start = (f32[2,2,192]{2,1,0:T(2,128)}, f32[2,2,192]{2,1,0:T(2,128)S(1)}, u32[]{:S(2)}, u32[]{:S(2)}) collective-permute-start(f32[2,2,192]{2,1,0:T(2,128)} %param.13), channel_id=1, source_target_pairs={{0,1},{1,2},{2,3},{4,5},{5,6},{6,7},{8,9},{9,10},{10,11},{12,13},{... | collective-permute-start | bytes 9224 | tf_op jit(solution)/shard_map/ppermute | solution.py:20
  3.0 6.2 %collective-permute-start.1 = (f32[2,2,192]{2,1,0:T(2,128)}, f32[2,2,192]{2,1,0:T(2,128)S(1)}, u32[]{:S(2)}, u32[]{:S(2)}) collective-permute-start(f32[2,2,192]{2,1,0:T(2,128)} %param.13), channel_id=1, source_target_pairs={{1,0},{2,1},{3,2},{5,4},{6,5},{7,6},{9,8},{10,9},{11,10},{13,12},{... | collective-permute-start | bytes 9224 | tf_op jit(solution)/shard_map/ppermute | solution.py:23
  4.3 1.5 copy-start.4
  7.7 0.7 copy-start.6
  9.2 0.7 copy-start.5
  9.9 6.9 %copy-start.1 = (f32[192,192]{1,0:T(8,128)S(1)}, f32[192,192]{1,0:T(8,128)}, u32[]{:S(2)}) copy-start(f32[192,192]{1,0:T(8,128)} %onsite_ref.1) | copy-start | bytes 442372
  9.9 6.9 %copy-start.2 = (f32[192,192]{1,0:T(8,128)S(1)}, f32[192,192]{1,0:T(8,128)}, u32[]{:S(2)}) copy-start(f32[192,192]{1,0:T(8,128)} %hop_ref.5) | copy-start | bytes 442372
  12.7 4.0 %collective-permute-start.2 = (f32[2,1,384]{2,1,0:T(1,128)S(1)}, f32[2,1,384]{2,1,0:T(1,128)S(1)}, u32[]{:S(2)}, u32[]{:S(2)}) collective-permute-start(f32[2,1,384]{2,1,0:T(1,128)S(1)} %get-tuple-element.70), channel_id=1, source_target_pairs={{0,4},{4,0},{8,12},{12,8},{16,20},{20,16},{24,28},{28,24},{1,5},{5... | collective-permute-start | bytes 9224 | tf_op jit(solution)/shard_map/ppermute | solution.py:36
  16.8 32.0 %copy-start.3 = (f32[2,2,2,192,128]{4,3,2,1,0:T(8,128)S(1)}, f32[2,2,2,192,128]{4,3,2,1,0:T(8,128)}, u32[]{:S(2)}) copy-start(f32[2,2,2,192,128]{4,3,2,1,0:T(8,128)} %param.8) | copy-start | bytes 2359300
  47.5 13.3 %collective-permute-start.4 = (f32[2,1,192,192]{3,2,1,0:T(8,128)S(1)}, f32[2,1,192,192]{3,2,1,0:T(8,128)S(1)}, u32[]{:S(2)}, u32[]{:S(2)}) collective-permute-start(f32[2,1,192,192]{3,2,1,0:T(8,128)S(1)} %get-tuple-element.42), channel_id=1, source_target_pairs={{8,0},{12,4},{16,8},{20,12},{24,16},{28,20},{9,1},{13,5},{17,9},{2... | collective-permute-start | bytes 884744 | tf_op jit(solution)/shard_map/ppermute | solution.py:31
  48.9 23.6 %collective-permute-start.3 = (f32[2,2,1,192,128]{4,3,1,2,0:T(8,128)S(1)}, f32[2,2,1,192,128]{4,3,1,2,0:T(8,128)S(1)}, u32[]{:S(2)}, u32[]{:S(2)}) collective-permute-start(f32[2,2,1,192,128]{4,3,1,2,0:T(8,128)S(1)} %get-tuple-element.68), channel_id=1, source_target_pairs={{0,4},{4,0},{8,12},{12,8},{16,20},{20,16},{24,28},{28,24},{1,5},{5... | collective-permute-start | bytes 1179656 | tf_op jit(solution)/shard_map/ppermute | solution.py:36
  51.0 25.5 %collective-permute-start.5 = (f32[2,1,192,192]{3,2,1,0:T(8,128)S(1)}, f32[2,1,192,192]{3,2,1,0:T(8,128)S(1)}, u32[]{:S(2)}, u32[]{:S(2)}) collective-permute-start(f32[2,1,192,192]{3,2,1,0:T(8,128)S(1)} %get-tuple-element.45), channel_id=1, source_target_pairs={{8,0},{12,4},{16,8},{20,12},{24,16},{28,20},{9,1},{13,5},{17,9},{2... | collective-permute-start | bytes 884744 | tf_op jit(solution)/shard_map/ppermute | solution.py:31
  75.2 14.4 %collective-permute-start.12 = (f32[2,1,192,128]{3,2,1,0:T(8,128)S(1)}, f32[2,1,192,128]{3,2,1,0:T(8,128)S(1)}, u32[]{:S(2)}, u32[]{:S(2)}) collective-permute-start(f32[2,1,192,128]{3,2,1,0:T(8,128)S(1)} %get-tuple-element.57), channel_id=1, source_target_pairs={{8,0},{12,4},{16,8},{20,12},{24,16},{28,20},{9,1},{13,5},{17,9},{2... | collective-permute-start | bytes 589832 | tf_op jit(solution)/shard_map/ppermute | solution.py:31
  77.3 16.3 %collective-permute-start.9 = (f32[2,1,192,192]{3,2,1,0:T(8,128)S(1)}, f32[2,1,192,192]{3,2,1,0:T(8,128)S(1)}, u32[]{:S(2)}, u32[]{:S(2)}) collective-permute-start(f32[2,1,192,192]{3,2,1,0:T(8,128)S(1)} %get-tuple-element.47), channel_id=1, source_target_pairs={{8,0},{12,4},{16,8},{20,12},{24,16},{28,20},{9,1},{13,5},{17,9},{2... | collective-permute-start | bytes 884744 | tf_op jit(solution)/shard_map/ppermute | solution.py:31
  78.6 19.0 %collective-permute-start.8 = (f32[2,1,192,192]{3,2,1,0:T(8,128)S(1)}, f32[2,1,192,192]{3,2,1,0:T(8,128)S(1)}, u32[]{:S(2)}, u32[]{:S(2)}) collective-permute-start(f32[2,1,192,192]{3,2,1,0:T(8,128)S(1)} %get-tuple-element.48), channel_id=1, source_target_pairs={{0,8},{4,12},{8,16},{12,20},{16,24},{20,28},{1,9},{5,13},{9,17},{1... | collective-permute-start | bytes 884744 | tf_op jit(solution)/shard_map/ppermute | solution.py:31
  84.2 17.9 %collective-permute-start.6 = (f32[2,1,192,192]{3,2,1,0:T(8,128)S(1)}, f32[2,1,192,192]{3,2,1,0:T(8,128)S(1)}, u32[]{:S(2)}, u32[]{:S(2)}) collective-permute-start(f32[2,1,192,192]{3,2,1,0:T(8,128)S(1)} %get-tuple-element.47), channel_id=1, source_target_pairs={{0,8},{4,12},{8,16},{12,20},{16,24},{20,28},{1,9},{5,13},{9,17},{1... | collective-permute-start | bytes 884744 | tf_op jit(solution)/shard_map/ppermute | solution.py:31
  88.1 14.1 %collective-permute-start.7 = (f32[2,1,192,192]{3,2,1,0:T(8,128)S(1)}, f32[2,1,192,192]{3,2,1,0:T(8,128)S(1)}, u32[]{:S(2)}, u32[]{:S(2)}) collective-permute-start(f32[2,1,192,192]{3,2,1,0:T(8,128)S(1)} %get-tuple-element.48), channel_id=1, source_target_pairs={{8,0},{12,4},{16,8},{20,12},{24,16},{28,20},{9,1},{13,5},{17,9},{2... | collective-permute-start | bytes 884744 | tf_op jit(solution)/shard_map/ppermute | solution.py:31
  90.1 32.3 %collective-permute-start.14 = (f32[2,1,192,128]{3,2,1,0:T(8,128)S(1)}, f32[2,1,192,128]{3,2,1,0:T(8,128)S(1)}, u32[]{:S(2)}, u32[]{:S(2)}) collective-permute-start(f32[2,1,192,128]{3,2,1,0:T(8,128)S(1)} %shard_map.103), channel_id=1, source_target_pairs={{8,0},{12,4},{16,8},{20,12},{24,16},{28,20},{9,1},{13,5},{17,9},{2... | collective-permute-start | bytes 589832 | tf_op jit(solution)/shard_map/ppermute | solution.py:31
  93.6 28.9 %collective-permute-start.13 = (f32[2,1,192,128]{3,2,1,0:T(8,128)S(1)}, f32[2,1,192,128]{3,2,1,0:T(8,128)S(1)}, u32[]{:S(2)}, u32[]{:S(2)}) collective-permute-start(f32[2,1,192,128]{3,2,1,0:T(8,128)S(1)} %shard_map.103), channel_id=1, source_target_pairs={{0,8},{4,12},{8,16},{12,20},{16,24},{20,28},{1,9},{5,13},{9,17},{1... | collective-permute-start | bytes 589832 | tf_op jit(solution)/shard_map/ppermute | solution.py:31
  115.5 15.0 %collective-permute-start.10 = (f32[2,1,192,192]{3,2,1,0:T(8,128)S(1)}, f32[2,1,192,192]{3,2,1,0:T(8,128)S(1)}, u32[]{:S(2)}, u32[]{:S(2)}) collective-permute-start(f32[2,1,192,192]{3,2,1,0:T(8,128)S(1)} %get-tuple-element.53), channel_id=1, source_target_pairs={{0,16},{4,20},{8,24},{12,28},{1,17},{5,21},{9,25},{13,29},{2,18},{... | collective-permute-start | bytes 884744 | tf_op jit(solution)/shard_map/ppermute | solution.py:31
  121.1 26.4 %collective-permute-start.11 = (f32[2,1,192,192]{3,2,1,0:T(8,128)S(1)}, f32[2,1,192,192]{3,2,1,0:T(8,128)S(1)}, u32[]{:S(2)}, u32[]{:S(2)}) collective-permute-start(f32[2,1,192,192]{3,2,1,0:T(8,128)S(1)} %get-tuple-element.54), channel_id=1, source_target_pairs={{16,0},{20,4},{24,8},{28,12},{17,1},{21,5},{25,9},{29,13},{18,2},{... | collective-permute-start | bytes 884744 | tf_op jit(solution)/shard_map/ppermute | solution.py:31
  123.7 36.3 %collective-permute-start.16 = (f32[2,1,192,128]{3,2,1,0:T(8,128)S(1)}, f32[2,1,192,128]{3,2,1,0:T(8,128)S(1)}, u32[]{:S(2)}, u32[]{:S(2)}) collective-permute-start(f32[2,1,192,128]{3,2,1,0:T(8,128)S(1)} %get-tuple-element.58), channel_id=1, source_target_pairs={{16,0},{20,4},{24,8},{28,12},{17,1},{21,5},{25,9},{29,13},{18,2},{... | collective-permute-start | bytes 589832 | tf_op jit(solution)/shard_map/ppermute | solution.py:31
  125.0 35.0 %collective-permute-start.15 = (f32[2,1,192,128]{3,2,1,0:T(8,128)S(1)}, f32[2,1,192,128]{3,2,1,0:T(8,128)S(1)}, u32[]{:S(2)}, u32[]{:S(2)}) collective-permute-start(f32[2,1,192,128]{3,2,1,0:T(8,128)S(1)} %get-tuple-element.58), channel_id=1, source_target_pairs={{0,16},{4,20},{8,24},{12,28},{1,17},{5,21},{9,25},{13,29},{2,18},{... | collective-permute-start | bytes 589832 | tf_op jit(solution)/shard_map/ppermute | solution.py:31
  161.7 4.5 %collective-permute-start.17 = (f32[2,1,192,128]{3,2,1,0:T(8,128)S(1)}, f32[2,1,192,128]{3,2,1,0:T(8,128)S(1)}, u32[]{:S(2)}, u32[]{:S(2)}) collective-permute-start(f32[2,1,192,128]{3,2,1,0:T(8,128)S(1)} %get-tuple-element.60.x3_ref), channel_id=1, source_target_pairs={{0,8},{4,12},{8,16},{12,20},{16,24},{20,28},{1,9},{5,13},{9,17},{1... | collective-permute-start | bytes 589832 | tf_op jit(solution)/shard_map/ppermute | solution.py:31
  167.0 6.9 %collective-permute-start.19 = (f32[2,1,192,128]{3,2,0,1:T(8,128)S(1)}, f32[2,1,192,128]{3,2,0,1:T(8,128)S(1)}, u32[]{:S(2)}, u32[]{:S(2)}) collective-permute-start(f32[2,1,192,128]{3,2,0,1:T(8,128)S(1)} %bitcast_select_fusion.2), channel_id=1, source_target_pairs={{0,4},{4,0},{8,12},{12,8},{16,20},{20,16},{24,28},{28,24},{1,5},{5... | collective-permute-start | bytes 589832 | tf_op jit(solution)/shard_map/ppermute | solution.py:36
  170.0 5.9 %collective-permute-start.18 = (f32[2,1,192,128]{3,2,0,1:T(8,128)S(1)}, f32[2,1,192,128]{3,2,0,1:T(8,128)S(1)}, u32[]{:S(2)}, u32[]{:S(2)}) collective-permute-start(f32[2,1,192,128]{3,2,0,1:T(8,128)S(1)} %bitcast_select_fusion.3), channel_id=1, source_target_pairs={{0,4},{4,0},{8,12},{12,8},{16,20},{20,16},{24,28},{28,24},{1,5},{5... | collective-permute-start | bytes 589832 | tf_op jit(solution)/shard_map/ppermute | solution.py:36
where the time goes:
time: 178 us
  Pallas kernels  77.8 us (44%)
  starting transfers between devices  46.7 us (26%)
  waiting for transfers between devices  41.6 us (23%)
  local copies, waits for them, and re-layouts  3.78 us (2%)
  other arithmetic  3.77 us (2%)
  matrix products  2.9 us (2%)
    pallas_call x13, Pallas kernels, run(): pl.pallas_call(kernel, out_shape=[jax.ShapeDtypeStruct(shape, jnp.float32...  77.8 us
    ppermute x14, starting transfers between devices, shifted(): return lax.ppermute(array, axis, pairs)  36.5 us
    ppermute x14, waiting for transfers between devices, shifted(): return lax.ppermute(array, axis, pairs)  34.7 us
    ppermute x4, waiting for transfers between devices, swapped(): return lax.ppermute(array, axis, [(i, i ^ 1) for i in range(count)])  6.89 us
    ppermute x4, starting transfers between devices, swapped(): return lax.ppermute(array, axis, [(i, i ^ 1) for i in range(count)])  6.64 us
  transfers between devices with their start and end apart: 20, of which 9 were waited for; matrix products, arithmetic and copies ran while one was open for 3% of the time, Pallas kernels for 25%

commit v1 on v0

--- a/solution.py
+++ b/solution.py
@@ -34,10 +34,6 @@
 def swapped(array, axis):
     count = lax.axis_size(axis)
     return lax.ppermute(array, axis, [(i, i ^ 1) for i in range(count)])
-
-
-def matmul_exact(left, right):
-    return jnp.matmul(left, right, precision=lax.Precision.HIGHEST)
 
 
 def halves(value):
@@ -248,8 +244,7 @@
 
 def local_kernel(
     onsite_ref, hop_ref, real_ref, imag_ref,
-    g0_ref, g1_ref, g2_ref, below_ref, above_ref, sb_ref, sa_ref,
-    out_pivot_ref, out_upper_ref, pivot_ref, lower_ref, state,
+    g0_ref, g1_ref, g2_ref, below_ref, above_ref, sb_ref, out_pivot_ref, pivot_ref, state,
 ):
     count = real_ref.shape[1]
     size = onsite_ref.shape[0]
@@ -282,22 +277,30 @@
         middle.append(minus(block(1, e), plus(real_dot(hop_t, g0h), real_dot(hop, g2t))))
     for e, g1 in enumerate(invert_all(state, middle)):
         put(g1_ref, g1, e)
-        below, above = take(below_ref, e), take(above_ref, e)
-        below_t, above_t = turned(below), turned(above)
+        below = take(below_ref, e)
         sb = complex_dot(g1, below)
-        sa = complex_dot(g1, above)
         put(sb_ref, sb, e)
-        put(sa_ref, sa, e)
-        put(out_pivot_ref, minus(take(out_pivot_ref, e), complex_dot(below_t, sb)), e)
-        put(pivot_ref, minus(take(pivot_ref, e), complex_dot(above_t, sa)), e)
-        lower = negative(complex_dot(above_t, sb))
-        put(lower_ref, lower, e)
-        put(out_upper_ref, turned(lower), e)
-
-
-def local_right_kernel(
-    hop_ref, g0_ref, g1_ref, g2_ref, below_ref, above_ref, right_ref,
-    z0_ref, z1_ref, z2_ref, out_ref, own_ref,
+        put(out_pivot_ref, minus(take(out_pivot_ref, e), complex_dot(turned(below), sb)), e)
+
+
+def put_pair(ref, right, square, e):
+    columns = right[0].shape[-1]
+    for part in range(2):
+        ref[part, e, :, :columns] = right[part]
+        ref[part, e, :, columns:] = square[part]
+
+
+def take_right(ref, columns, e):
+    return ref[0, e, :, :columns], ref[1, e, :, :columns]
+
+
+def take_square(ref, columns, e):
+    return ref[0, e, :, columns:], ref[1, e, :, columns:]
+
+
+def local_rest_kernel(
+    hop_ref, joined_ref, g0_ref, g1_ref, g2_ref, below_ref, above_ref, sb_ref, partial_ref,
+    right_ref, z0_ref, z1_ref, z2_ref, sa_ref, pivot_ref, lower_ref, own_ref, out_ref,
 ):
     hop = hop_ref[...]
     hop_t = hop.T
@@ -305,25 +308,31 @@
         b0, b1, b2, b3 = (
             (right_ref[slab, 0, e], right_ref[slab, 1, e]) for slab in range(4)
         )
+        g1 = take(g1_ref, e)
+        above = take(above_ref, e)
+        above_t = turned(above)
+        sa = complex_dot(g1, above)
+        put(sa_ref, sa, e)
+        put(pivot_ref, minus(take(partial_ref, e), complex_dot(above_t, sa)), e)
+        lower = tuple(
+            jnp.where(joined_ref[...] > 0, -part, 0.0)
+            for part in complex_dot(above_t, take(sb_ref, e))
+        )
+        put(lower_ref, lower, e)
         z0 = complex_dot(take(g0_ref, e), b0)
         z2 = complex_dot(take(g2_ref, e), b2)
         b1 = plus(b1, plus(real_dot(hop_t, z0), real_dot(hop, z2)))
-        z1 = complex_dot(take(g1_ref, e), b1)
+        z1 = complex_dot(g1, b1)
         put(z0_ref, z0, e)
         put(z1_ref, z1, e)
         put(z2_ref, z2, e)
-        put(
+        put_pair(
             out_ref,
             minus(real_dot(hop, z0), complex_dot(turned(take(below_ref, e)), z1)),
+            turned(lower),
             e,
         )
-        put(
-            own_ref,
-            minus(
-                plus(b3, real_dot(hop_t, z2)), complex_dot(turned(take(above_ref, e)), z1)
-            ),
-            e,
-        )
+        put(own_ref, minus(plus(b3, real_dot(hop_t, z2)), complex_dot(above_t, z1)), e)
 
 
 def first_kernel(own_ref, more_ref, pivot_ref, g_ref, state):
@@ -348,35 +357,99 @@
         put(g_ref, inverse[e], e)
 
 
-def scale_kernel(g_ref, lower_ref, upper_ref, xl_ref, xu_ref):
+def last_kernel(old_ref, link_ref, other_ref, pivot_ref, g_ref, state):
+    count = old_ref.shape[1]
+    for e in range(count):
+        change = complex_dot(take(link_ref, e), take(other_ref, e))
+        put(pivot_ref, minus(take(old_ref, e), change), e)
+    inverse = invert_all(state, [take(pivot_ref, e) for e in range(count)])
+    for e in range(count):
+        put(g_ref, inverse[e], e)
+
+
+def scale_kernel(g_ref, lower_ref, rest_ref, xl_ref, xu_ref):
+    columns = rest_ref.shape[-1] - lower_ref.shape[-1]
     for e in range(g_ref.shape[1]):
         g = take(g_ref, e)
         put(xl_ref, complex_dot(g, take(lower_ref, e)), e)
-        put(xu_ref, complex_dot(g, take(upper_ref, e)), e)
-
-
-def product_kernel(left_ref, right_ref, out_ref):
-    for e in range(left_ref.shape[1]):
-        put(out_ref, complex_dot(take(left_ref, e), take(right_ref, e)), e)
-
-
-def coupling_kernel(lower_ref, upper_ref, below_ref, above_ref, new_lower_ref, new_upper_ref):
-    for e in range(lower_ref.shape[1]):
-        put(new_lower_ref, negative(complex_dot(take(lower_ref, e), take(below_ref, e))), e)
-        put(new_upper_ref, negative(complex_dot(take(upper_ref, e), take(above_ref, e))), e)
-
-
-def right_kernel(
-    g_ref, lower_ref, upper_ref, below_ref, above_ref, right_ref, new_ref, x_ref
+        put(xu_ref, complex_dot(g, take_square(rest_ref, columns, e)), e)
+
+
+def rest_kernel(g_ref, xl_ref, xu_ref, own_ref, rest_ref, right_ref, up_ref, down_ref):
+    columns = own_ref.shape[-1]
+    for e in range(g_ref.shape[1]):
+        right = plus(take(own_ref, e), take_right(rest_ref, columns, e))
+        put(right_ref, right, e)
+        x = complex_dot(take(g_ref, e), right)
+        put_pair(up_ref, x, take(xl_ref, e), e)
+        put_pair(down_ref, x, take(xu_ref, e), e)
+
+
+def rescale_kernel(
+    g_ref, lower_ref, upper_ref, below_ref, above_ref,
+    new_lower_ref, new_upper_ref, xl_ref, xu_ref,
 ):
-    for e in range(lower_ref.shape[1]):
-        change = plus(
-            complex_dot(take(lower_ref, e), take(below_ref, e)),
-            complex_dot(take(upper_ref, e), take(above_ref, e)),
-        )
-        new = minus(take(right_ref, e), change)
-        put(new_ref, new, e)
-        put(x_ref, complex_dot(take(g_ref, e), new), e)
+    columns = below_ref.shape[-1] - lower_ref.shape[-1]
+    for e in range(g_ref.shape[1]):
+        g = take(g_ref, e)
+        lower = negative(complex_dot(take(lower_ref, e), take_square(below_ref, columns, e)))
+        upper = negative(complex_dot(take(upper_ref, e), take_square(above_ref, columns, e)))
+        put(new_lower_ref, lower, e)
+        put(new_upper_ref, upper, e)
+        put(xl_ref, complex_dot(g, lower), e)
+        put(xu_ref, complex_dot(g, upper), e)
+
+
+def rescale_last_kernel(g_ref, lower_ref, upper_ref, below_ref, above_ref, link_ref, x_ref):
+    columns = below_ref.shape[-1] - lower_ref.shape[-1]
+    for e in range(g_ref.shape[1]):
+        link = negative(
+            plus(
+                complex_dot(take(lower_ref, e), take_square(below_ref, columns, e)),
+                complex_dot(take(upper_ref, e), take_square(above_ref, columns, e)),
+            )
+        )
+        put(link_ref, link, e)
+        put(x_ref, complex_dot(take(g_ref, e), link), e)
+
+
+def right_change(lower_ref, upper_ref, below_ref, above_ref, e):
+    columns = below_ref.shape[-1] - lower_ref.shape[-1]
+    return plus(
+        complex_dot(take(lower_ref, e), take_right(below_ref, columns, e)),
+        complex_dot(take(upper_ref, e), take_right(above_ref, columns, e)),
+    )
+
+
+def rest_again_kernel(
+    g_ref, lower_ref, upper_ref, below_ref, above_ref, old_ref, xl_ref, xu_ref,
+    right_ref, up_ref, down_ref,
+):
+    for e in range(g_ref.shape[1]):
+        right = minus(
+            take(old_ref, e), right_change(lower_ref, upper_ref, below_ref, above_ref, e)
+        )
+        put(right_ref, right, e)
+        x = complex_dot(take(g_ref, e), right)
+        put_pair(up_ref, x, take(xl_ref, e), e)
+        put_pair(down_ref, x, take(xu_ref, e), e)
+
+
+def rest_last_kernel(
+    g_ref, lower_ref, upper_ref, below_ref, above_ref, old_ref, right_ref, x_ref
+):
+    for e in range(g_ref.shape[1]):
+        right = minus(
+            take(old_ref, e), right_change(lower_ref, upper_ref, below_ref, above_ref, e)
+        )
+        put(right_ref, right, e)
+        put(x_ref, complex_dot(take(g_ref, e), right), e)
+
+
+def final_kernel(g_ref, link_ref, other_ref, right_ref, x_ref):
+    for e in range(g_ref.shape[1]):
+        change = complex_dot(take(link_ref, e), take(other_ref, e))
+        put(x_ref, complex_dot(take(g_ref, e), minus(take(right_ref, e), change)), e)
 
 
 def middle_kernel(z1_ref, sb_ref, sa_ref, previous_ref, x3_ref, x1_ref):
@@ -428,11 +501,11 @@
         above = (all_points == own_points + energy_count + phonon_shift[mode]).astype(jnp.float32)
         below = (all_points == own_points + energy_count - phonon_shift[mode]).astype(jnp.float32)
         weights = weights + coupling[mode] * (above + below)
-    damping = jnp.einsum("ek,skb->seb", weights, widened, precision=lax.Precision.HIGHEST)
+    damping = jnp.sum(weights[None, :, :, None] * widened[:, None], axis=2)
     chosen = (
         slab_profile[:, None] == jnp.arange(potential_table.shape[0], dtype=jnp.int32)[None, :]
-    ).astype(jnp.float32)
-    potential = matmul_exact(chosen, potential_table)
+    )
+    potential = jnp.sum(jnp.where(chosen[..., None], potential_table[None], 0.0), axis=1)
 
     def exchanged(array, axis):
         low = lax.slice_in_dim(array, 0, half, axis=axis)
@@ -464,37 +537,43 @@
     imag_diag = broadening + damping
     square = (2, half, orbitals, orbitals)
     tall = (2, half, orbitals, source.shape[-1])
-    g0, g1, g2, below, above, sb, sa, out_pivot, out_upper, pivot, lower = run(
+    columns = source.shape[-1]
+    wide = (2, half, orbitals, columns + orbitals)
+    count = lax.axis_size("slab") // 2
+    if count < 4 or count & (count - 1):
+        raise ValueError("unsupported mesh")
+    g0, g1, g2, below, above, sb, out_pivot, partial = run(
         local_kernel,
-        [square] * 11,
+        [square] * 8,
         [onsite_block, hop, real_diag, imag_diag],
         orbitals,
         2 * half,
         30,
     )
+    joined = jnp.full((1, orbitals), place // 2, jnp.int32)
     more = shifted(out_pivot, "slab", -2)
-    z0, z1, z2, out_right, right_now = run(
-        local_right_kernel, [tall] * 5, [hop, g0, g1, g2, below, above, right]
-    )
-    upper = shifted(out_upper, "slab", -2)
-    right_now = (right_now, shifted(out_right, "slab", -2))
-    count = lax.axis_size("slab") // 2
+    z0, z1, z2, sa, pivot, lower, right_now, out_rest = run(
+        local_rest_kernel,
+        [tall, tall, tall, square, square, square, tall, wide],
+        [hop, joined, g0, g1, g2, below, above, sb, partial, right],
+    )
+    more, out_rest = lax.optimization_barrier((more, out_rest))
+    rest = shifted(out_rest, "slab", -2)
     pivot, inverse = run(first_kernel, [square] * 2, [pivot, more], orbitals, half, 14)
-    right_now = right_now[0] + right_now[1]
-    scaled_right = None
-    for level in range((count - 1).bit_length()):
-        distance = 2 << level
-        last = distance >= count
-        x_lower, x_upper = run(scale_kernel, [square] * 2, [inverse, lower, upper])
-        below_upper = shifted(x_upper, "slab", distance)
-        above_lower = shifted(x_lower, "slab", -distance)
-        if scaled_right is None:
-            (scaled_right,) = run(product_kernel, [tall], [inverse, right_now])
-        if not last:
-            below_lower = shifted(x_lower, "slab", distance)
-            above_upper = shifted(x_upper, "slab", -distance)
-        below_right = shifted(scaled_right, "slab", distance)
-        above_right = shifted(scaled_right, "slab", -distance)
+    x_lower, x_upper = run(scale_kernel, [square] * 2, [inverse, lower, rest])
+    upper = rest[..., columns:]
+    distance = 2
+    below_upper = shifted(x_upper, "slab", distance)
+    above_lower = shifted(x_lower, "slab", -distance)
+    right_now, up, down = run(
+        rest_kernel, [tall, wide, wide], [inverse, x_lower, x_upper, right_now, rest]
+    )
+    while True:
+        below_upper, above_lower, up, down = lax.optimization_barrier(
+            (below_upper, above_lower, up, down)
+        )
+        below_rest = shifted(up, "slab", distance)
+        above_rest = shifted(down, "slab", -distance)
         pivot, inverse = run(
             level_kernel,
             [square] * 2,
@@ -503,18 +582,34 @@
             half,
             14,
         )
-        right_now, scaled_right = run(
-            right_kernel,
-            [tall] * 2,
-            [inverse, lower, upper, below_right, above_right, right_now],
-        )
-        if not last:
-            lower, upper = run(
-                coupling_kernel, [square] * 2, [lower, upper, below_lower, above_upper]
-            )
-    if scaled_right is None:
-        (scaled_right,) = run(product_kernel, [tall], [inverse, right_now])
-    x3 = scaled_right
+        distance *= 2
+        if distance == count:
+            break
+        new_lower, new_upper, x_lower, x_upper = run(
+            rescale_kernel, [square] * 4, [inverse, lower, upper, below_rest, above_rest]
+        )
+        below_upper = shifted(x_upper, "slab", distance)
+        above_lower = shifted(x_lower, "slab", -distance)
+        right_now, up, down = run(
+            rest_again_kernel,
+            [tall, wide, wide],
+            [inverse, lower, upper, below_rest, above_rest, right_now, x_lower, x_upper],
+        )
+        lower, upper = new_lower, new_upper
+    partners = [(i, (i + count) % (2 * count)) for i in range(2 * count)]
+    link, x = run(
+        rescale_last_kernel, [square] * 2, [inverse, lower, upper, below_rest, above_rest]
+    )
+    other = lax.ppermute(x, "slab", partners)
+    right_now, x_right = run(
+        rest_last_kernel,
+        [tall] * 2,
+        [inverse, lower, upper, below_rest, above_rest, right_now],
+    )
+    other, x_right = lax.optimization_barrier((other, x_right))
+    other_right = lax.ppermute(x_right, "slab", partners)
+    pivot, inverse = run(last_kernel, [square] * 2, [pivot, link, other], orbitals, half, 14)
+    (x3,) = run(final_kernel, [tall], [inverse, link, other_right, right_now])
     previous = shifted(x3, "slab", 2)
     (x1,) = run(middle_kernel, [tall], [z1, sb, sa, previous, x3])
     first = swapped(jnp.where(upper_half, x1, x3), "slab")

time: 178 us -> 166 us (0.933)
  starting transfers between devices: 46.7 us -> 26 us
  waiting for transfers between devices: 41.6 us -> 47.8 us
  other arithmetic: 3.77 us -> 8.65 us
  matrix products: 2.9 us -> 0 us
    ppermute x14 -> x7, starting transfers between devices: 36.5 us -> 16.6 us  [shifted(): return lax.ppermute(array, axis, pairs)]
    ppermute x0 -> x2, waiting for transfers between devices: none -> 15.2 us  [the longest x1 15.2 us: per_device(): other = lax.ppermute(x, 'slab', partners)]
    ppermute x14 -> x7, waiting for transfers between devices: 34.7 us -> 25.7 us  [shifted(): return lax.ppermute(array, axis, pairs)]
    dot_general x2 -> x0, matrix products: 2.9 us -> none  [the longest x1 2.72 us: per_device(): jnp.einsum('ek,skb->seb', weights, widened, precision=lax.Precision.HIGHEST)]
    add x1, other arithmetic: 0.02 us -> 2.57 us  [per_device(): weights = weights + coupling[mode] * (above + below)]
    ppermute x4, starting transfers between devices: 6.64 us -> 4.67 us  [swapped(): return lax.ppermute(array, axis, [(i, i ^ 1) for i in range(count)])]
    pallas_call x13 -> x12, Pallas kernels: 77.8 us -> 77.8 us  [run(): pl.pallas_call(kernel, out_shape=[jax.ShapeDtypeStruct(shape, jnp.float32...]
  transfers between devices with their start and end apart: 20 -> 15, of which waited for: 9 -> 10; matrix products, arithmetic and copies ran while one was open for 3% -> 6% of each run, Pallas kernels for 25% -> 44%
where the time goes in v1:
time: 166 us; the launch traced here: 165 us
  Pallas kernels  77.8 us (47%)
  waiting for transfers between devices  47.8 us (29%)
  starting transfers between devices  26 us (16%)
  other arithmetic  8.65 us (5%)
  local copies, waits for them, and re-layouts  3.8 us (2%)
    pallas_call x12, Pallas kernels, run(): pl.pallas_call(kernel, out_shape=[jax.ShapeDtypeStruct(shape, jnp.float32...  77.8 us
    ppermute x7, waiting for transfers between devices, shifted(): return lax.ppermute(array, axis, pairs)  25.7 us
    ppermute x7, starting transfers between devices, shifted(): return lax.ppermute(array, axis, pairs)  16.6 us
    ppermute x1, waiting for transfers between devices, per_device(): other = lax.ppermute(x, 'slab', partners)  15.2 us
    ppermute x4, waiting for transfers between devices, swapped(): return lax.ppermute(array, axis, [(i, i ^ 1) for i in range(count)])  6.84 us
    ppermute x4, starting transfers between devices, swapped(): return lax.ppermute(array, axis, [(i, i ^ 1) for i in range(count)])  4.67 us
  transfers between devices with their start and end apart: 15, of which 10 were waited for; matrix products, arithmetic and copies ran while one was open for 6% of the time, Pallas kernels for 44%

profile of v1, /device:TPU:0, one launch (start us, length us, event | category | flops | bytes accessed | tf_op | source)
XLA Modules:
  0.0 165.0 jit_solution(2798566010201330441)
XLA Ops:
  0.6 2.4 %collective-permute-start = (f32[2,2,192]{2,1,0:T(2,128)}, f32[2,2,192]{2,1,0:T(2,128)S(1)}, u32[]{:S(2)}, u32[]{:S(2)}) collective-permute-start(f32[2,2,192]{2,1,0:T(2,128)} %param.13), channel_id=1, source_target_pairs={{0,1},{1,2},{2,3},{4,5},{5,6},{6,7},{8,9},{9,10},{10,11},{12,13},{... | collective-permute-start | bytes 9224 | tf_op jit(solution)/shard_map/ppermute | solution.py:20
  3.0 1.3 collective-permute-start.1
  4.3 1.5 fusion.13
  5.8 0.7 fusion.4
  6.5 0.6 fusion.6
  7.1 0.7 fusion.8
  7.7 0.7 fusion.10
  8.4 0.7 fusion.12
  9.2 2.6 %multiply_add_fusion = f32[2,6]{0,1:T(8,128)S(1)} fusion(s32[2]{0:T(128)S(1)} %get-tuple-element.100, s32[2]{0:T(128)S(1)} %get-tuple-element.101, f32[]{:T(128)} %bitcast.6, s32[2]{0:T(128)S(1)} %get-tuple-element.102, s32[2]{0:T(128)S(1)} %get-tuple-element.103, f32[]{:T(128)} %bitcast.4, s32[2]{0:T(128)S(1)} %get-tuple-element.104, ...), kind=kLoop, calls=%fused_computation.22 | loop fusion | flops 324 | bytes 128 | tf_op jit(solution)/shard_map/add | solution.py:503
  11.9 0.6 copy-done.4
  12.8 2.4 %collective-permute-start.2 = (f32[2,1,384]{2,1,0:T(1,128)S(1)}, f32[2,1,384]{2,1,0:T(1,128)S(1)}, u32[]{:S(2)}, u32[]{:S(2)}) collective-permute-start(f32[2,1,384]{2,1,0:T(1,128)S(1)} %get-tuple-element.88), channel_id=1, source_target_pairs={{0,4},{4,0},{8,12},{12,8},{16,20},{20,16},{24,28},{28,24},{1,5},{5... | collective-permute-start | bytes 9224 | tf_op jit(solution)/shard_map/ppermute | solution.py:36
  15.2 1.2 bitcast_select_fusion.1
  16.4 0.2 collective-permute-start.3
  16.5 0.2 collective-permute-done.2
  16.8 29.7 %shard_map.95 = (f32[2,1,192,192]{3,2,1,0:T(8,128)S(1)}, f32[2,1,192,192]{3,2,1,0:T(8,128)S(1)}, f32[2,1,192,192]{3,2,1,0:T(8,128)S(1)}, f32[2,1,192,192]{3,2,1,...) custom-call(f32[192,192]{1,0:T(8,128)S(1)} %copy-done, ...), custom_call_target="tpu_custom_call" | custom-call | flops 30000001024 | bytes 1000000 | tf_op jit(solution)/shard_map/pallas_call | solution.py:232
  46.6 1.3 collective-permute-start.4
  47.9 0.9 fusion.right_ref
  48.9 4.9 %shard_map.96 = (f32[2,1,192,128]{3,2,1,0:T(8,128)S(1)}, f32[2,1,192,128]{3,2,1,0:T(8,128)S(1)}, f32[2,1,192,128]{3,2,1,0:T(8,128)S(1)}, f32[2,1,192,192]{3,2,1,...) custom-call(f32[192,192]{1,0:T(8,128)S(1)} %copy-done.1, ...), custom_call_target="tpu_custom_call" | custom-call | flops 2000000000 | bytes 1000000 | tf_op jit(solution)/shard_map/pallas_call | solution.py:232
  53.7 5.8 %collective-permute-done.4.more_ref = f32[2,1,192,192]{3,2,1,0:T(8,128)S(1)} collective-permute-done((f32[2,1,192,192]{3,2,1,0:T(8,128)S(1)}, f32[2,1,192,192]{3,2,1,0:T(8,128)S(1)}, u32[]{:S(2)}, u32[]{:S(2)}) %collective-permute-start.4) | collective-permute-done | bytes 294944 | tf_op jit(solution)/shard_map/ppermute | solution.py:31
  59.6 1.3 collective-permute-start.5
  60.8 11.7 %shard_map.97 = (f32[2,1,192,192]{3,2,1,0:T(8,128)S(1)}, f32[2,1,192,192]{3,2,1,0:T(8,128)S(1)}) custom-call(f32[2,1,192,192]{3,2,1,0:T(8,128)S(1)} %get-tuple-element.51.own_ref, f32[2,1,192,192]{3,2,1,0:T(8,128)S(1)} %collective-permute-done.4.more_ref), custom_call_target="tpu_custom_call" | custom-call | flops 14000000000 | bytes 1000000 | tf_op jit(solution)/shard_map/pallas_call | solution.py:232
  72.6 5.2 %collective-permute-done.5.rest_ref = f32[2,1,192,320]{3,2,1,0:T(8,128)S(1)} collective-permute-done((f32[2,1,192,320]{3,2,1,0:T(8,128)S(1)}, f32[2,1,192,320]{3,2,1,0:T(8,128)S(1)}, u32[]{:S(2)}, u32[]{:S(2)}) %collective-permute-start.5) | collective-permute-done | bytes 491552 | tf_op jit(solution)/shard_map/ppermute | solution.py:31
  77.8 0.8 shard_map.98
  78.6 3.7 %collective-permute-start.6 = (f32[2,1,192,192]{3,2,1,0:T(8,128)S(1)}, f32[2,1,192,192]{3,2,1,0:T(8,128)S(1)}, u32[]{:S(2)}, u32[]{:S(2)}) collective-permute-start(f32[2,1,192,192]{3,2,1,0:T(8,128)S(1)} %get-tuple-element.59.xu_ref), channel_id=1, source_target_pairs={{0,8},{4,12},{8,16},{12,20},{16,24},{20,28},{1,9},{5,13},{9,17},{1... | collective-permute-start | bytes 884744 | tf_op jit(solution)/shard_map/ppermute | solution.py:31
  82.2 1.5 collective-permute-start.7
  83.7 0.5 shard_map.99
  84.2 6.0 %collective-permute-done.6.below_ref = f32[2,1,192,192]{3,2,1,0:T(8,128)S(1)} collective-permute-done((f32[2,1,192,192]{3,2,1,0:T(8,128)S(1)}, f32[2,1,192,192]{3,2,1,0:T(8,128)S(1)}, u32[]{:S(2)}, u32[]{:S(2)}) %collective-permute-start.6) | collective-permute-done | bytes 294944 | tf_op jit(solution)/shard_map/ppermute | solution.py:31
  90.2 4.1 %collective-permute-done.7.above_ref = f32[2,1,192,192]{3,2,1,0:T(8,128)S(1)} collective-permute-done((f32[2,1,192,192]{3,2,1,0:T(8,128)S(1)}, f32[2,1,192,192]{3,2,1,0:T(8,128)S(1)}, u32[]{:S(2)}, u32[]{:S(2)}) %collective-permute-start.7) | collective-permute-done | bytes 294944 | tf_op jit(solution)/shard_map/ppermute | solution.py:31
  94.4 3.5 %collective-permute-start.8 = (f32[2,1,192,320]{3,2,1,0:T(8,128)S(1)}, f32[2,1,192,320]{3,2,1,0:T(8,128)S(1)}, u32[]{:S(2)}, u32[]{:S(2)}) collective-permute-start(f32[2,1,192,320]{3,2,1,0:T(8,128)S(1)} %get-tuple-element.68), channel_id=1, source_target_pairs={{0,8},{4,12},{8,16},{12,20},{16,24},{20,28},{1,9},{5,13},{9,17},{1... | collective-permute-start | bytes 1474568 | tf_op jit(solution)/shard_map/ppermute | solution.py:31
  97.9 1.3 collective-permute-start.9
  99.2 12.5 %shard_map.100 = (f32[2,1,192,192]{3,2,1,0:T(8,128)S(1)}, f32[2,1,192,192]{3,2,1,0:T(8,128)S(1)}) custom-call(f32[2,1,192,192]{3,2,1,0:T(8,128)S(1)} %get-tuple-element.55.old_ref, f32[2,1,192,192]{3,2,1,0:T(8,128)S(1)} %get-tuple-element.56.lower_ref, f32[2,1,192,192]{3,2,1,0:T(8,128)S(1)} %slice.76.upper_ref, ...), custom_call_target="tpu_custom_call" | custom-call | flops 14000000000 | bytes 1000000 | tf_op jit(solution)/shard_map/pallas_call | solution.py:232
  111.6 1.4 collective-permute-done.9.above_ref
  113.0 1.3 shard_map.101
  114.3 1.0 collective-permute-start.10
  115.3 1.2 shard_map.102
  116.5 15.2 %collective-permute-done.10.other_ref = f32[2,1,192,192]{3,2,1,0:T(8,128)S(1)} collective-permute-done((f32[2,1,192,192]{3,2,1,0:T(8,128)S(1)}, f32[2,1,192,192]{3,2,1,0:T(8,128)S(1)}, u32[]{:S(2)}, u32[]{:S(2)}) %collective-permute-start.10) | collective-permute-done | bytes 294944 | tf_op jit(solution)/shard_map/ppermute | solution.py:603
  131.8 12.2 %shard_map.103 = (f32[2,1,192,192]{3,2,1,0:T(8,128)}, f32[2,1,192,192]{3,2,1,0:T(8,128)S(1)}) custom-call(f32[2,1,192,192]{3,2,1,0:T(8,128)S(1)} %get-tuple-element.66.old_ref, f32[2,1,192,192]{3,2,1,0:T(8,128)S(1)} %get-tuple-element.70.link_ref, f32[2,1,192,192]{3,2,1,0:T(8,128)S(1)} %collective-permute-done.10.other_ref), custom_call_target="tpu_custom_call" | custom-call | flops 14000000000 | bytes 1000000 | tf_op jit(solution)/shard_map/pallas_call | solution.py:232
  143.9 0.9 shard_map.104.x3_ref
  144.9 4.2 %collective-permute-start.12 = (f32[2,1,192,128]{3,2,1,0:T(8,128)S(1)}, f32[2,1,192,128]{3,2,1,0:T(8,128)S(1)}, u32[]{:S(2)}, u32[]{:S(2)}) collective-permute-start(f32[2,1,192,128]{3,2,1,0:T(8,128)S(1)} %shard_map.104.x3_ref), channel_id=1, source_target_pairs={{0,8},{4,12},{8,16},{12,20},{16,24},{20,28},{1,9},{5,13},{9,17},{1... | collective-permute-start | bytes 589832 | tf_op jit(solution)/shard_map/ppermute | solution.py:31
  149.0 3.2 %collective-permute-done.12.previous_ref = f32[2,1,192,128]{3,2,1,0:T(8,128)S(1)} collective-permute-done((f32[2,1,192,128]{3,2,1,0:T(8,128)S(1)}, f32[2,1,192,128]{3,2,1,0:T(8,128)S(1)}, u32[]{:S(2)}, u32[]{:S(2)}) %collective-permute-start.12) | collective-permute-done | bytes 196640 | tf_op jit(solution)/shard_map/ppermute | solution.py:31
  152.2 0.8 shard_map.105.x1_ref
  153.0 1.4 shard_map.106
  154.5 1.6 collective-permute-start.13
  156.1 0.5 collective-permute-start.14
  156.6 4.5 %collective-permute-done.13 = f32[2,1,192,128]{3,2,0,1:T(8,128)S(1)} collective-permute-done((f32[2,1,192,128]{3,2,0,1:T(8,128)S(1)}, f32[2,1,192,128]{3,2,0,1:T(8,128)S(1)}, u32[]{:S(2)}, u32[]{:S(2)}) %collective-permute-start.13) | collective-permute-done | bytes 196640 | tf_op jit(solution)/shard_map/ppermute | solution.py:36
  161.1 2.1 %collective-permute-done.14 = f32[2,1,192,128]{3,2,0,1:T(8,128)S(1)} collective-permute-done((f32[2,1,192,128]{3,2,0,1:T(8,128)S(1)}, f32[2,1,192,128]{3,2,0,1:T(8,128)S(1)}, u32[]{:S(2)}, u32[]{:S(2)}) %collective-permute-start.14) | collective-permute-done | bytes 196640 | tf_op jit(solution)/shard_map/ppermute | solution.py:36
  163.3 0.9 copy.25
  164.2 0.8 fusion.2
  (31 shorter events, 0.7 us)
Async XLA Ops:
  0.6 11.2 %collective-permute-start = (f32[2,2,192]{2,1,0:T(2,128)}, f32[2,2,192]{2,1,0:T(2,128)S(1)}, u32[]{:S(2)}, u32[]{:S(2)}) collective-permute-start(f32[2,2,192]{2,1,0:T(2,128)} %param.13), channel_id=1, source_target_pairs={{0,1},{1,2},{2,3},{4,5},{5,6},{6,7},{8,9},{9,10},{10,11},{12,13},{... | collective-permute-start | bytes 9224 | tf_op jit(solution)/shard_map/ppermute | solution.py:20
  3.0 8.9 %collective-permute-start.1 = (f32[2,2,192]{2,1,0:T(2,128)}, f32[2,2,192]{2,1,0:T(2,128)S(1)}, u32[]{:S(2)}, u32[]{:S(2)}) collective-permute-start(f32[2,2,192]{2,1,0:T(2,128)} %param.13), channel_id=1, source_target_pairs={{1,0},{2,1},{3,2},{5,4},{6,5},{7,6},{9,8},{10,9},{11,10},{13,12},{... | collective-permute-start | bytes 9224 | tf_op jit(solution)/shard_map/ppermute | solution.py:23
  7.7 0.7 copy-start.3
  8.4 0.7 copy-start.5
  9.2 2.6 %copy-start.2 = (f32[16,192]{1,0:T(8,128)S(1)}, f32[16,192]{1,0:T(8,128)}, u32[]{:S(2)}) copy-start(f32[16,192]{1,0:T(8,128)} %param.11) | copy-start | bytes 36868
  11.8 0.7 copy-start.4
  12.7 4.1 %copy-start = (f32[192,192]{1,0:T(8,128)S(1)}, f32[192,192]{1,0:T(8,128)}, u32[]{:S(2)}) copy-start(f32[192,192]{1,0:T(8,128)} %onsite_ref.1) | copy-start | bytes 442372
  12.7 4.1 %copy-start.1 = (f32[192,192]{1,0:T(8,128)S(1)}, f32[192,192]{1,0:T(8,128)}, u32[]{:S(2)}) copy-start(f32[192,192]{1,0:T(8,128)} %hop_ref.5) | copy-start | bytes 442372
  12.8 4.0 %collective-permute-start.2 = (f32[2,1,384]{2,1,0:T(1,128)S(1)}, f32[2,1,384]{2,1,0:T(1,128)S(1)}, u32[]{:S(2)}, u32[]{:S(2)}) collective-permute-start(f32[2,1,384]{2,1,0:T(1,128)S(1)} %get-tuple-element.88), channel_id=1, source_target_pairs={{0,4},{4,0},{8,12},{12,8},{16,20},{20,16},{24,28},{28,24},{1,5},{5... | collective-permute-start | bytes 9224 | tf_op jit(solution)/shard_map/ppermute | solution.py:36
  16.4 31.5 %collective-permute-start.3 = (f32[2,2,1,192,128]{4,3,1,2,0:T(8,128)S(1)}, f32[2,2,1,192,128]{4,3,1,2,0:T(8,128)S(1)}, u32[]{:S(2)}, u32[]{:S(2)}) collective-permute-start(f32[2,2,1,192,128]{4,3,1,2,0:T(8,128)S(1)} %get-tuple-element.86), channel_id=1, source_target_pairs={{0,4},{4,0},{8,12},{12,8},{16,20},{20,16},{24,28},{28,24},{1,5},{5... | collective-permute-start | bytes 1179656 | tf_op jit(solution)/shard_map/ppermute | solution.py:36
  46.6 13.0 %collective-permute-start.4 = (f32[2,1,192,192]{3,2,1,0:T(8,128)S(1)}, f32[2,1,192,192]{3,2,1,0:T(8,128)S(1)}, u32[]{:S(2)}, u32[]{:S(2)}) collective-permute-start(f32[2,1,192,192]{3,2,1,0:T(8,128)S(1)} %get-tuple-element.52), channel_id=1, source_target_pairs={{8,0},{12,4},{16,8},{20,12},{24,16},{28,20},{9,1},{13,5},{17,9},{2... | collective-permute-start | bytes 884744 | tf_op jit(solution)/shard_map/ppermute | solution.py:31
  59.6 18.2 %collective-permute-start.5 = (f32[2,1,192,320]{3,2,1,0:T(8,128)S(1)}, f32[2,1,192,320]{3,2,1,0:T(8,128)S(1)}, u32[]{:S(2)}, u32[]{:S(2)}) collective-permute-start(f32[2,1,192,320]{3,2,1,0:T(8,128)S(1)} %get-tuple-element.57), channel_id=1, source_target_pairs={{8,0},{12,4},{16,8},{20,12},{24,16},{28,20},{9,1},{13,5},{17,9},{2... | collective-permute-start | bytes 1474568 | tf_op jit(solution)/shard_map/ppermute | solution.py:31
  78.6 11.7 %collective-permute-start.6 = (f32[2,1,192,192]{3,2,1,0:T(8,128)S(1)}, f32[2,1,192,192]{3,2,1,0:T(8,128)S(1)}, u32[]{:S(2)}, u32[]{:S(2)}) collective-permute-start(f32[2,1,192,192]{3,2,1,0:T(8,128)S(1)} %get-tuple-element.59.xu_ref), channel_id=1, source_target_pairs={{0,8},{4,12},{8,16},{12,20},{16,24},{20,28},{1,9},{5,13},{9,17},{1... | collective-permute-start | bytes 884744 | tf_op jit(solution)/shard_map/ppermute | solution.py:31
  82.2 12.1 %collective-permute-start.7 = (f32[2,1,192,192]{3,2,1,0:T(8,128)S(1)}, f32[2,1,192,192]{3,2,1,0:T(8,128)S(1)}, u32[]{:S(2)}, u32[]{:S(2)}) collective-permute-start(f32[2,1,192,192]{3,2,1,0:T(8,128)S(1)} %get-tuple-element.60.xl_ref), channel_id=1, source_target_pairs={{8,0},{12,4},{16,8},{20,12},{24,16},{28,20},{9,1},{13,5},{17,9},{2... | collective-permute-start | bytes 884744 | tf_op jit(solution)/shard_map/ppermute | solution.py:31
  94.4 17.3 %collective-permute-start.8 = (f32[2,1,192,320]{3,2,1,0:T(8,128)S(1)}, f32[2,1,192,320]{3,2,1,0:T(8,128)S(1)}, u32[]{:S(2)}, u32[]{:S(2)}) collective-permute-start(f32[2,1,192,320]{3,2,1,0:T(8,128)S(1)} %get-tuple-element.68), channel_id=1, source_target_pairs={{0,8},{4,12},{8,16},{12,20},{16,24},{20,28},{1,9},{5,13},{9,17},{1... | collective-permute-start | bytes 1474568 | tf_op jit(solution)/shard_map/ppermute | solution.py:31
  97.9 15.1 %collective-permute-start.9 = (f32[2,1,192,320]{3,2,1,0:T(8,128)S(1)}, f32[2,1,192,320]{3,2,1,0:T(8,128)S(1)}, u32[]{:S(2)}, u32[]{:S(2)}) collective-permute-start(f32[2,1,192,320]{3,2,1,0:T(8,128)S(1)} %get-tuple-element.69), channel_id=1, source_target_pairs={{8,0},{12,4},{16,8},{20,12},{24,16},{28,20},{9,1},{13,5},{17,9},{2... | collective-permute-start | bytes 1474568 | tf_op jit(solution)/shard_map/ppermute | solution.py:31
  114.3 17.5 %collective-permute-start.10 = (f32[2,1,192,192]{3,2,1,0:T(8,128)S(1)}, f32[2,1,192,192]{3,2,1,0:T(8,128)S(1)}, u32[]{:S(2)}, u32[]{:S(2)}) collective-permute-start(f32[2,1,192,192]{3,2,1,0:T(8,128)S(1)} %get-tuple-element.71), channel_id=1, source_target_pairs={{0,16},{4,20},{8,24},{12,28},{16,0},{20,4},{24,8},{28,12},{1,17},{... | collective-permute-start | bytes 884744 | tf_op jit(solution)/shard_map/ppermute | solution.py:603
  131.8 12.2 %collective-permute-start.11 = (f32[2,1,192,128]{3,2,1,0:T(8,128)S(1)}, f32[2,1,192,128]{3,2,1,0:T(8,128)S(1)}, u32[]{:S(2)}, u32[]{:S(2)}) collective-permute-start(f32[2,1,192,128]{3,2,1,0:T(8,128)S(1)} %get-tuple-element.76), channel_id=1, source_target_pairs={{0,16},{4,20},{8,24},{12,28},{16,0},{20,4},{24,8},{28,12},{1,17},{... | collective-permute-start | bytes 589832 | tf_op jit(solution)/shard_map/ppermute | solution.py:610
  144.9 7.3 %collective-permute-start.12 = (f32[2,1,192,128]{3,2,1,0:T(8,128)S(1)}, f32[2,1,192,128]{3,2,1,0:T(8,128)S(1)}, u32[]{:S(2)}, u32[]{:S(2)}) collective-permute-start(f32[2,1,192,128]{3,2,1,0:T(8,128)S(1)} %shard_map.104.x3_ref), channel_id=1, source_target_pairs={{0,8},{4,12},{8,16},{12,20},{16,24},{20,28},{1,9},{5,13},{9,17},{1... | collective-permute-start | bytes 589832 | tf_op jit(solution)/shard_map/ppermute | solution.py:31
  154.5 6.6 %collective-permute-start.13 = (f32[2,1,192,128]{3,2,0,1:T(8,128)S(1)}, f32[2,1,192,128]{3,2,0,1:T(8,128)S(1)}, u32[]{:S(2)}, u32[]{:S(2)}) collective-permute-start(f32[2,1,192,128]{3,2,0,1:T(8,128)S(1)} %bitcast_select_fusion.3), channel_id=1, source_target_pairs={{0,4},{4,0},{8,12},{12,8},{16,20},{20,16},{24,28},{28,24},{1,5},{5... | collective-permute-start | bytes 589832 | tf_op jit(solution)/shard_map/ppermute | solution.py:36
  156.1 7.2 %collective-permute-start.14 = (f32[2,1,192,128]{3,2,0,1:T(8,128)S(1)}, f32[2,1,192,128]{3,2,0,1:T(8,128)S(1)}, u32[]{:S(2)}, u32[]{:S(2)}) collective-permute-start(f32[2,1,192,128]{3,2,0,1:T(8,128)S(1)} %bitcast_select_fusion.2), channel_id=1, source_target_pairs={{0,4},{4,0},{8,12},{12,8},{16,20},{20,16},{24,28},{28,24},{1,5},{5... | collective-permute-start | bytes 589832 | tf_op jit(solution)/shard_map/ppermute | solution.py:36
